TPU v7x, 128 devices: a whole 4x4x4 slice. The times are simulated.
128 devices in a mesh: dp: 4 (over x_lo, core), expert: 32 (over z, y, x_hi).
Axes of the slice: x: 4 (x_hi: 2, x_lo: 2; x = x_hi * 2 + x_lo), y: 4, z: 4, core: 2. Of those that a mesh axis runs over, the one named last changes fastest.
Arguments:
- hidden: bfloat16 [131072, 8, 1536], P(('dp', 'expert')), may hold values from -96 to 96, as said below
- expert_ids: int32 [131072, 8], P(('dp', 'expert')), may hold values from 0 to 127, all different within a row; in each aligned block of 1024 rows (0 to 1023, 1024 to 2047, ...) at most 96 rows name the same one
Outputs:
- factors: float32 [32, 1536, 1536], P('expert', 'dp')
Inputs may be any that keep to these rules, and one draw needn't show every extreme that they name: `hidden`: entries are real-valued activations. `expert_ids`: each token names 8 different experts; among the 1024 tokens of one device no expert is named by more than 96 tokens; every expert is named by some token.
All inputs are finite; a program needn't handle non-finite values.
Results may differ from a plain program's by a relative error of at most 0.0003.
Values may be sent and summed in bfloat16 or wider, within the bound.
No kernel may reach another device: no remote copies, remote signals or barrier semaphores. Data moves between devices by JAX's collectives and lax.ppermute only.
A program may use at most 192 MiB of HBM per device.

v0:
```python
import jax
import jax.numpy as jnp
from jax import lax
from jax.sharding import PartitionSpec as P

EXP_DEV = 4


damp_share = 0.01
highest = lax.Precision.HIGHEST


def broadcast(value, axis, root):
    mine = lax.axis_index(axis) == root
    return lax.psum(jnp.where(mine, value, jnp.zeros_like(value)), axis)


def shards(hidden, expert_ids):
    tokens_here, top_k, features = hidden.shape
    owners = lax.axis_size("expert")
    capacity = 3 * tokens_here * top_k // (2 * EXP_DEV * owners)
    flat_ids = expert_ids.reshape(-1)
    owner_of = flat_ids // EXP_DEV
    in_flight = flat_ids % EXP_DEV == 0
    owner_range = jnp.arange(owners, dtype=jnp.int32)
    chosen = ((owner_of[:, None] == owner_range[None, :]) & in_flight[:, None]).astype(jnp.int32)
    slot_rank = jnp.sum(jnp.cumsum(chosen, axis=0) * chosen, axis=1) - 1
    target = jnp.where(in_flight, owner_of * capacity + slot_rank, owners * capacity)
    outgoing = jnp.zeros((owners * capacity, features), jnp.bfloat16)
    outgoing = outgoing.at[target].set(hidden.reshape(-1, features), mode="drop")
    sent_counts = jnp.sum(chosen, axis=0).astype(jnp.bfloat16)
    arrived, arrived_counts = (
        lax.all_to_all(
            outgoing.reshape(owners, capacity, features),
            "expert",
            split_axis=0,
            concat_axis=0,
            tiled=True,
        ),
        lax.all_to_all(sent_counts, "expert", split_axis=0, concat_axis=0, tiled=True),
    )
    received = arrived.reshape(-1, features)
    count_here = jnp.sum(arrived_counts.astype(jnp.float32))
    square_here = jnp.sum(jnp.square(received.astype(jnp.float32)))
    count_all, square_all = lax.psum((count_here, square_here), "dp")
    blocks = lax.axis_size("dp")
    block_rows = features // blocks
    my_index = lax.axis_index("dp")
    contract = (((0,), (0,)), ((), ()))
    gram_block = lax.psum_scatter(
        lax.dot_general(received, received, contract, preferred_element_type=jnp.float32),
        "dp",
        scatter_dimension=0,
        tiled=True,
    )
    scaling = 2.0 / count_all
    damping = damp_share * scaling * square_all / features
    col_index = jnp.arange(features, dtype=jnp.int32)[None, :]
    row_index = my_index * block_rows + jnp.arange(block_rows, dtype=jnp.int32)[:, None]
    remain = scaling * gram_block + jnp.where(col_index == row_index, damping, 0.0)
    factor = jnp.zeros((block_rows, features), jnp.float32)
    for section_idx in range(blocks):
        start_col = section_idx * block_rows
        panel_rows = broadcast(remain, "dp", section_idx)[:, start_col:]
        corner = jnp.linalg.cholesky(panel_rows[:, :block_rows])
        solved = jax.scipy.linalg.solve_triangular(corner, panel_rows, lower=True)
        offset = jnp.clip(
            (my_index - section_idx) * block_rows, 0, panel_rows.shape[1] - block_rows
        )
        lower_block = lax.dynamic_slice_in_dim(solved, offset, block_rows, 1).T
        factor = factor.at[:, start_col : start_col + block_rows].set(
            jnp.where(my_index >= section_idx, lower_block, 0.0)
        )
        below_mask = jnp.where(my_index > section_idx, 1.0, 0.0).astype(jnp.float32)
        update = jnp.dot(lower_block, solved, precision=highest, preferred_element_type=jnp.float32)
        remain = remain.at[:, start_col:].add(-below_mask * update)
    return factor[None]


def solution(mesh):
    placed = (P(("dp", "expert"), None, None), P(("dp", "expert"), None))
    return jax.shard_map(
        shards, mesh=mesh, in_specs=placed, out_specs=P("expert", "dp", None), check_vma=False
    )
```

profile of v0, /device:TPU:1, one launch (start us, length us, event | category | flops | bytes accessed | tf_op | source)
XLA Modules:
  0.0 1042.1 jit_solution(2577072479701398396)
XLA Ops:
  20.8 44.0 %scatter_custom_fusion = bf16[3072,1536]{1,0:T(8,128)(2,1)} fusion(s32[8192]{0:T(1024)S(1)} %bitcast.207, bf16[1024,8,1536]{2,1,0:T(8,128)(2,1)} %param.19, bf16[]{:T(256)} %constant.364.clone.1), kind=kCustom, calls=%fused_computation.9 | custom fusion | bytes 34603008 | tf_op jit(solution)/shard_map/scatter | solution.py:30
  64.7 119.8 %all_to_all.11 = bf16[32,96,1536]{2,1,0:T(8,128)(2,1)S(1)} all-to-all(bf16[32,96,1536]{2,1,0:T(8,128)(2,1)} %bitcast.202), channel_id=1, replica_groups=mesh['dp'=4,'expert'=32] {'expert'}, dimensions={0} | all-to-all | bytes 18874368 | tf_op jit(solution)/shard_map/all_to_all | solution.py:33
  188.2 17.4 %convolution_bitcast_fusion = f32[1536,1536]{0,1:T(8,128)} fusion(bf16[32,96,1536]{2,1,0:T(8,128)(2,1)S(1)} %all_to_all.11), kind=kOutput, calls=%fused_computation.12 | convolution fusion | flops 14495514624 | bytes 18874368 | tf_op jit(solution)/shard_map/dot_general | solution.py:51
  239.1 51.5 %reduce-scatter.2.cloned.1.call-done = f32[384,1536]{0,1:T(8,128)} async-done(((f32[1536,1536]{0,1:T(8,128)}), f32[384,1536]{0,1:T(8,128)}) %reduce-scatter.2.cloned.1.call-update) | async-done | bytes 2359312 | tf_op jit(solution)/shard_map/reduce_scatter | solution.py:50
  294.4 62.6 %all-reduce.8.cloned.1.call-done = f32[384,1536]{0,1:T(8,128)} async-done(((f32[384,1536]{0,1:T(8,128)}), f32[384,1536]{0,1:T(8,128)}) %all-reduce.8.cloned.1.call-update) | async-done | bytes 2359312 | tf_op jit(solution)/shard_map/psum | solution.py:15
  359.4 11.7 %cholesky.338 = f32[128,128]{1,0:T(8,128)S(1)} custom-call(f32[128,128]{1,0:T(8,128)S(1)} %cholesky.546), custom_call_target="Cholesky" | custom-call | tf_op jit(solution)/shard_map/jit(cholesky)/cholesky | solution.py:65
  373.4 11.3 %custom-call.40 = f32[1,128,128]{1,2,0:T(8,128)} custom-call(f32[1,128,128]{2,1,0:T(8,128)} %get-tuple-element.201), custom_call_target="InvertDiagBlocksLowerTriangular" | custom-call | tf_op jit(solution)/shard_map/jit(cholesky)/cholesky | solution.py:65
  387.4 13.2 %cholesky.357 = f32[128,128]{1,0:T(8,128)} custom-call(f32[128,128]{1,0:T(8,128)} %cholesky.550), custom_call_target="Cholesky" | custom-call | tf_op jit(solution)/shard_map/jit(cholesky)/cholesky | solution.py:65
  402.0 11.4 %custom-call.41 = f32[1,128,128]{1,2,0:T(8,128)} custom-call(f32[1,128,128]{2,1,0:T(8,128)} %get-tuple-element.198), custom_call_target="InvertDiagBlocksLowerTriangular" | custom-call | tf_op jit(solution)/shard_map/jit(cholesky)/cholesky | solution.py:65
  415.5 12.5 %cholesky.376 = f32[128,128]{1,0:T(8,128)S(1)} custom-call(f32[128,128]{1,0:T(8,128)} %convolution_subtract_fusion.15), custom_call_target="Cholesky" | custom-call | tf_op jit(solution)/shard_map/jit(cholesky)/cholesky | solution.py:65
  437.0 29.9 %custom-call.30 = f32[3,128,128]{1,2,0:T(8,128)S(1)} custom-call(f32[3,128,128]{2,1,0:T(8,128)S(1)} %get-tuple-element.105), custom_call_target="InvertDiagBlocksLowerTriangular" | custom-call | tf_op jit(solution)/shard_map/jit(_solve_triangular)/triangular_solve | solution.py:66
  482.5 62.7 %all-reduce.10.cloned.1.call-done = f32[384,1536]{0,1:T(8,128)} async-done(((f32[384,1536]{0,1:T(8,128)}), f32[384,1536]{0,1:T(8,128)}) %all-reduce.10.cloned.1.call-update) | async-done | bytes 2359312 | tf_op jit(solution)/shard_map/psum | solution.py:15
  547.7 11.7 %cholesky.391 = f32[128,128]{1,0:T(8,128)S(1)} custom-call(f32[128,128]{1,0:T(8,128)S(1)} %cholesky.554), custom_call_target="Cholesky" | custom-call | tf_op jit(solution)/shard_map/jit(cholesky)/cholesky | solution.py:65
  561.5 11.3 %custom-call.42 = f32[1,128,128]{1,2,0:T(8,128)} custom-call(f32[1,128,128]{2,1,0:T(8,128)} %get-tuple-element.194), custom_call_target="InvertDiagBlocksLowerTriangular" | custom-call | tf_op jit(solution)/shard_map/jit(cholesky)/cholesky | solution.py:65
  575.5 13.2 %cholesky.410 = f32[128,128]{1,0:T(8,128)} custom-call(f32[128,128]{1,0:T(8,128)} %cholesky.558), custom_call_target="Cholesky" | custom-call | tf_op jit(solution)/shard_map/jit(cholesky)/cholesky | solution.py:65
  591.4 11.6 %custom-call.43 = f32[1,128,128]{1,2,0:T(8,128)} custom-call(f32[1,128,128]{2,1,0:T(8,128)} %get-tuple-element.191), custom_call_target="InvertDiagBlocksLowerTriangular" | custom-call | tf_op jit(solution)/shard_map/jit(cholesky)/cholesky | solution.py:65
  605.1 12.5 %cholesky.429 = f32[128,128]{1,0:T(8,128)S(1)} custom-call(f32[128,128]{1,0:T(8,128)} %convolution_subtract_fusion.14), custom_call_target="Cholesky" | custom-call | tf_op jit(solution)/shard_map/jit(cholesky)/cholesky | solution.py:65
  625.9 29.5 %custom-call.31 = f32[3,128,128]{1,2,0:T(8,128)S(1)} custom-call(f32[3,128,128]{2,1,0:T(8,128)S(1)} %get-tuple-element.113), custom_call_target="InvertDiagBlocksLowerTriangular" | custom-call | tf_op jit(solution)/shard_map/jit(_solve_triangular)/triangular_solve | solution.py:66
  671.1 62.5 %all-reduce.12.cloned.1.call-done = f32[384,1536]{0,1:T(8,128)} async-done(((f32[384,1536]{0,1:T(8,128)}), f32[384,1536]{0,1:T(8,128)}) %all-reduce.12.cloned.1.call-update) | async-done | bytes 2359312 | tf_op jit(solution)/shard_map/psum | solution.py:15
  736.1 11.7 %cholesky.444 = f32[128,128]{1,0:T(8,128)S(1)} custom-call(f32[128,128]{1,0:T(8,128)S(1)} %cholesky.562), custom_call_target="Cholesky" | custom-call | tf_op jit(solution)/shard_map/jit(cholesky)/cholesky | solution.py:65
  749.9 11.3 %custom-call.44 = f32[1,128,128]{1,2,0:T(8,128)} custom-call(f32[1,128,128]{2,1,0:T(8,128)} %get-tuple-element.187), custom_call_target="InvertDiagBlocksLowerTriangular" | custom-call | tf_op jit(solution)/shard_map/jit(cholesky)/cholesky | solution.py:65
  763.9 13.2 %cholesky.463 = f32[128,128]{1,0:T(8,128)} custom-call(f32[128,128]{1,0:T(8,128)} %cholesky.566), custom_call_target="Cholesky" | custom-call | tf_op jit(solution)/shard_map/jit(cholesky)/cholesky | solution.py:65
  779.9 11.6 %custom-call.45 = f32[1,128,128]{1,2,0:T(8,128)} custom-call(f32[1,128,128]{2,1,0:T(8,128)} %get-tuple-element.184), custom_call_target="InvertDiagBlocksLowerTriangular" | custom-call | tf_op jit(solution)/shard_map/jit(cholesky)/cholesky | solution.py:65
  793.5 12.5 %cholesky.482 = f32[128,128]{1,0:T(8,128)S(1)} custom-call(f32[128,128]{1,0:T(8,128)} %convolution_subtract_fusion.13), custom_call_target="Cholesky" | custom-call | tf_op jit(solution)/shard_map/jit(cholesky)/cholesky | solution.py:65
  814.3 29.5 %custom-call.32 = f32[3,128,128]{1,2,0:T(8,128)S(1)} custom-call(f32[3,128,128]{2,1,0:T(8,128)S(1)} %get-tuple-element.121), custom_call_target="InvertDiagBlocksLowerTriangular" | custom-call | tf_op jit(solution)/shard_map/jit(_solve_triangular)/triangular_solve | solution.py:66
  862.6 55.2 %all-reduce.14.cloned.1.call-done = f32[384,1536]{0,1:T(8,128)} async-done(((f32[384,1536]{0,1:T(8,128)}), f32[384,1536]{0,1:T(8,128)}) %all-reduce.14.cloned.1.call-update) | async-done | bytes 2359312 | tf_op jit(solution)/shard_map/psum | solution.py:15
  920.2 11.7 %cholesky.497 = f32[128,128]{1,0:T(8,128)S(1)} custom-call(f32[128,128]{1,0:T(8,128)S(1)} %cholesky.570), custom_call_target="Cholesky" | custom-call | tf_op jit(solution)/shard_map/jit(cholesky)/cholesky | solution.py:65
  934.1 11.3 %custom-call.46 = f32[1,128,128]{1,2,0:T(8,128)} custom-call(f32[1,128,128]{2,1,0:T(8,128)} %get-tuple-element.180), custom_call_target="InvertDiagBlocksLowerTriangular" | custom-call | tf_op jit(solution)/shard_map/jit(cholesky)/cholesky | solution.py:65
  948.0 13.2 %cholesky.516 = f32[128,128]{1,0:T(8,128)} custom-call(f32[128,128]{1,0:T(8,128)} %cholesky.574), custom_call_target="Cholesky" | custom-call | tf_op jit(solution)/shard_map/jit(cholesky)/cholesky | solution.py:65
  964.1 11.5 %custom-call.47 = f32[1,128,128]{1,2,0:T(8,128)} custom-call(f32[1,128,128]{2,1,0:T(8,128)} %get-tuple-element.177), custom_call_target="InvertDiagBlocksLowerTriangular" | custom-call | tf_op jit(solution)/shard_map/jit(cholesky)/cholesky | solution.py:65
  977.5 12.5 %cholesky.535 = f32[128,128]{1,0:T(8,128)S(1)} custom-call(f32[128,128]{1,0:T(8,128)} %convolution_subtract_fusion.12), custom_call_target="Cholesky" | custom-call | tf_op jit(solution)/shard_map/jit(cholesky)/cholesky | solution.py:65
  998.5 29.5 %custom-call.33 = f32[3,128,128]{1,2,0:T(8,128)S(1)} custom-call(f32[3,128,128]{2,1,0:T(8,128)S(1)} %get-tuple-element.129), custom_call_target="InvertDiagBlocksLowerTriangular" | custom-call | tf_op jit(solution)/shard_map/jit(_solve_triangular)/triangular_solve | solution.py:66
  (217 shorter events, 206.7 us)
Async XLA Ops:
  6.5 284.0 %reduce-scatter.2.cloned.1.call-start = ((), (), s32[]{:S(2)}) async-start(), calls=%async_computation.3 | async-start | bytes 11796480 | tf_op jit(solution)/shard_map/reduce_scatter | solution.py:50
  184.5 3.7 copy-start
  206.4 12.6 %all-to-all-start = ((bf16[32,1,1]{2,1,0:T(2,128)(2,1)}), bf16[32,1,1]{2,1,0:T(2,128)(2,1)S(1)}, u32[]{:S(2)}, u32[]{:S(2)}) async-start(bf16[32,1,1]{2,1,0:T(2,128)(2,1)} %copy.25), calls=%async_computation | async-start | bytes 32768 | tf_op jit(solution)/shard_map/all_to_all | solution.py:40
  210.5 146.5 %all-reduce.8.cloned.1.call-start = ((), (), s32[]{:S(2)}) async-start(), calls=%async_computation.4 | async-start | bytes 4718592 | tf_op jit(solution)/shard_map/psum | solution.py:15
  294.1 251.1 %all-reduce.10.cloned.1.call-start = ((), (), s32[]{:S(2)}) async-start(), calls=%async_computation.5 | async-start | bytes 4718592 | tf_op jit(solution)/shard_map/psum | solution.py:15
  371.1 0.6 copy-start.11
  372.4 94.5 %copy-start.6 = (f32[384,1536]{0,1:T(8,128)S(1)}, f32[384,1536]{0,1:T(8,128)}, u32[]{:S(2)}) copy-start(f32[384,1536]{0,1:T(8,128)} %all-reduce.8.cloned.1.call-done) | copy-start | bytes 7077892
  386.1 0.7 copy-start.10
  473.7 1.7 copy-start.5
  475.4 7.1 copy-start.3
  482.5 251.2 %all-reduce.12.cloned.1.call-start = ((), (), s32[]{:S(2)}) async-start(), calls=%async_computation.6 | async-start | bytes 4718592 | tf_op jit(solution)/shard_map/psum | solution.py:15
  559.4 0.6 copy-start.12
  574.2 0.6 copy-start.7
  664.0 4.0 copy-start.4
  668.1 1.2 copy-start.1
  670.9 246.9 %all-reduce.14.cloned.1.call-start = ((), (), s32[]{:S(2)}) async-start(), calls=%async_computation.7 | async-start | bytes 4718592 | tf_op jit(solution)/shard_map/psum | solution.py:15
  747.8 0.6 copy-start.13
  762.6 0.6 copy-start.8
  847.6 3.2 copy-start.2
  931.9 0.6 copy-start.14
  946.8 0.7 copy-start.9
Sparse Core Ops, SparseCore 0:
  205.8 84.7 reduce-scatter.1
  294.2 62.6 all-reduce.7
  482.6 62.5 all-reduce.9
  671.0 62.5 all-reduce.11
  855.1 62.5 all-reduce.13
where the time goes:
time: 1050 us; the launch traced here: 1040 us
  other arithmetic  416 us (40%)
  waiting for transfers between devices  303 us (29%)
  blocking collectives  129 us (12%)
  local copies, waits for them, and re-layouts  95.2 us (9%)
  matrix products  71.9 us (7%)
  between operations  22.9 us (2%)
    another operation x43, other arithmetic, shards(): corner = jnp.linalg.cholesky(panel_rows[:, :block_rows])  257 us
    psum x4, waiting for transfers between devices, broadcast(): return lax.psum(jnp.where(mine, value, jnp.zeros_like(value)), axis)  243 us
    all_to_all x1, blocking collectives, shards(): lax.all_to_all(outgoing.reshape(owners, capacity, features), 'expert', sp...  120 us
    another operation x12, other arithmetic, shards(): solved = jax.scipy.linalg.solve_triangular(corner, panel_rows, lower=True)  119 us
    reduce_scatter x1, waiting for transfers between devices, shards(): lax.psum_scatter(lax.dot_general(received, received, contract, preferred_...  51.5 us
    scatter x1, local copies, waits for them, and re-layouts, shards(): outgoing.at[target].set(hidden.reshape(-1, features), mode='drop')  44 us
    another operation x20, matrix products, shards(): solved = jax.scipy.linalg.solve_triangular(corner, panel_rows, lower=True)  27.4 us
    another operation x37, local copies, waits for them, and re-layouts  23.5 us
  transfers between devices with their start and end apart: 6, of which 6 were waited for; matrix products, arithmetic and copies ran while one was open for 2% of the time, Pallas kernels for 0%

commit v1 on v0

v1 whole, which is shorter than its diff:
```python
import functools

import jax
import jax.numpy as jnp
from jax import lax
from jax.experimental import pallas as pl
from jax.experimental.pallas import tpu as pltpu
from jax.sharding import PartitionSpec as P

EXP_DEV = 4
WIDTH = 128
damp_share = 0.01
f32 = jnp.float32
bf16 = jnp.bfloat16


def split(x):
    high = x.astype(bf16)
    rest = x - high.astype(f32)
    middle = rest.astype(bf16)
    return high, middle, (rest - middle.astype(f32)).astype(bf16)


def left_terms(x):
    h, m, l = split(x)
    return jnp.concatenate([h, h, m, m, h, l], 1)


def right_terms(x):
    h, m, l = split(x)
    return jnp.concatenate([h, m, h, m, l, h], 1)


def dot_nt(a, b):
    return lax.dot_general(a, b, (((1,), (1,)), ((), ())), preferred_element_type=f32)


def reciprocal(x):
    r = pl.reciprocal(x, approx=True)
    r = r * (2.0 - x * r)
    return r * (2.0 - x * r)


def over_lanes(x, j):
    return jnp.broadcast_to(x[:, j : j + 1], (8, 128))


def over_rows(x, i):
    return jnp.broadcast_to(x[i : i + 1, :], x.shape)


def eliminate(rows):
    count = len(rows)
    wide = lambda v: jnp.concatenate([v, v], axis=1)
    rows = list(rows)
    sub = lax.broadcasted_iota(jnp.int32, (8, 128), 0)
    for m in range(count):
        group = rows[m]
        cols = [over_lanes(group, 8 * m + l) for l in range(8)]
        cell = [[over_rows(cols[l], i) if i >= l else None for l in range(8)] for i in range(8)]
        below = [[over_lanes(rows[t], 8 * m + l) for l in range(8)] for t in range(m + 1, count)]
        inverse, pivots, diagonal = [], [], None
        for j in range(8):
            d = cell[j][j]
            r = reciprocal(d)
            inverse.append(r)
            diagonal = d if diagonal is None else jnp.where(sub == j, d, diagonal)
            pairs = [(i, l) for i in range(j + 1, 8) for l in range(j + 1, i + 1)]
            products = [cell[i][j] * cell[l][j] for i, l in pairs]
            for (i, l), product in zip(pairs, products):
                cell[i][l] = cell[i][l] - product * r
            pivot = over_rows(group, j)
            pivots.append(pivot)
            group = group - wide(jnp.where(sub > j, cols[j] * r, 0.0)) * pivot
            for l in range(j + 1, 8):
                u = cell[l][j] * r
                cols[l] = cols[l] - cols[j] * u
                for b in below:
                    b[l] = b[l] - b[j] * u
        for b, t in zip(below, range(m + 1, count)):
            total = rows[t]
            for j in range(8):
                total = total - wide(b[j] * inverse[j]) * pivots[j]
            rows[t] = total
        rows[m] = group * wide(lax.rsqrt(diagonal))
    return rows


def factor_kernel(size, parts, count_ref, place_ref, *refs):
    gram_refs = refs[:parts]
    out_ref, work, inv, left, right = refs[parts:]
    steps = size // WIDTH
    share = size // parts
    for c in range(parts):
        for t in range(c * share, size, 128):
            work[t : t + 128, c * share : (c + 1) * share] = gram_refs[c][t - c * share : t - c * share + 128, :]
    eye = (
        lax.broadcasted_iota(jnp.int32, (128, 128), 0) == lax.broadcasted_iota(jnp.int32, (128, 128), 1)
    ).astype(f32)
    trace = jnp.zeros((128, 128), f32)
    for t in range(0, size, 128):
        trace = trace + work[t : t + 128, t : t + 128] * eye
    damping = damp_share / size * jnp.sum(trace)
    for t in range(0, size, 128):
        work[t : t + 128, t : t + 128] += eye * damping

    def step(k, carry):
        start = pl.multiple_of(k * WIDTH, WIDTH)
        rows = [
            jnp.concatenate([work[pl.ds(start + t, 8), pl.ds(start, WIDTH)], eye[t : t + 8]], 1)
            for t in range(0, WIDTH, 8)
        ]
        for t, row in enumerate(eliminate(rows)):
            inv[8 * t : 8 * t + 8, :] = row[:, WIDTH:]
        inverse_terms = right_terms(inv[...])
        for k_here in range(steps):

            @pl.when(k == k_here)
            def _(k_here=k_here):
                first = k_here * WIDTH
                below = first + WIDTH
                panel = dot_nt(left_terms(work[first:, first:below]), inverse_terms)
                work[first:, first:below] = panel
                if below < size:
                    left[below:, :] = left_terms(panel[WIDTH:])
                    right[below:, :] = right_terms(panel[WIDTH:])
                col = below
                while col < size:
                    wide = 256 if col % 256 == 0 else 128
                    work[col:, col : col + wide] -= dot_nt(left[col:, :], right[col : col + wide, :])
                    col += wide

        return carry

    lax.fori_loop(0, steps, step, 0)
    scale = jnp.sqrt(2.0 / count_ref[0])
    base = pl.multiple_of(place_ref[0] * share, share)
    for t in range(0, share, 64):
        row_index = base + t + lax.broadcasted_iota(jnp.int32, (64, size), 0)
        col_index = lax.broadcasted_iota(jnp.int32, (64, size), 1)
        out_ref[t : t + 64, :] = jnp.where(row_index >= col_index, work[pl.ds(base + t, 64), :] * scale, 0.0)


def factor(grams, count, place):
    size = grams[0].shape[0]
    parts = len(grams)
    scalar = pl.BlockSpec(memory_space=pltpu.SMEM)
    whole = pl.BlockSpec(memory_space=pltpu.VMEM)
    return pl.pallas_call(
        functools.partial(factor_kernel, size, parts),
        out_shape=jax.ShapeDtypeStruct((size // parts, size), f32),
        in_specs=[scalar, scalar] + [whole] * parts,
        out_specs=whole,
        scratch_shapes=[
            pltpu.VMEM((size, size), f32),
            pltpu.VMEM((WIDTH, WIDTH), f32),
            pltpu.VMEM((size, 6 * WIDTH), bf16),
            pltpu.VMEM((size, 6 * WIDTH), bf16),
        ],
        compiler_params=pltpu.CompilerParams(vmem_limit_bytes=56 * 2**20),
        name="factor",
    )(count, place, *grams)


def shards(hidden, expert_ids):
    tokens_here, top_k, features = hidden.shape
    owners = lax.axis_size("expert")
    capacity = 3 * tokens_here * top_k // (2 * EXP_DEV * owners)
    flat_ids = expert_ids.reshape(-1)
    owner_of = flat_ids // EXP_DEV
    in_flight = flat_ids % EXP_DEV == 0
    owner_range = jnp.arange(owners, dtype=jnp.int32)
    chosen = ((owner_of[:, None] == owner_range[None, :]) & in_flight[:, None]).astype(jnp.int32)
    counts = lax.psum(jnp.sum(chosen, axis=0).astype(f32), ("dp", "expert"))
    slot_rank = jnp.sum(jnp.cumsum(chosen, axis=0) * chosen, axis=1) - 1
    target = jnp.where(in_flight, owner_of * capacity + slot_rank, owners * capacity)
    outgoing = jnp.zeros((owners * capacity, features), bf16)
    outgoing = outgoing.at[target].set(hidden.reshape(-1, features), mode="drop")
    arrived = lax.all_to_all(
        outgoing.reshape(owners, capacity, features), "expert", split_axis=0, concat_axis=0, tiled=True
    )
    received = arrived.reshape(-1, features)
    parts = lax.axis_size("dp")
    share = features // parts
    place = lax.axis_index("dp")
    core = place % 2
    grams = []
    for c in range(parts):
        gram = lax.dot_general(
            received[:, c * share :],
            received[:, c * share : (c + 1) * share],
            (((0,), (0,)), ((), ())),
            preferred_element_type=f32,
        )
        half = gram.shape[0] // 2
        mine = lax.dynamic_slice_in_dim(gram, core * half, half, 0)
        other = lax.dynamic_slice_in_dim(gram, (1 - core) * half, half, 0)
        mine = mine + lax.ppermute(other, "dp", [(i, i ^ 1) for i in range(parts)])
        mine = mine + lax.ppermute(mine, "dp", [(i, i ^ 2) for i in range(parts)])
        other = lax.ppermute(mine, "dp", [(i, i ^ 1) for i in range(parts)])
        first = jnp.where(core == 0, mine, other)
        second = jnp.where(core == 0, other, mine)
        grams.append(jnp.concatenate([first, second], 0))
    count = lax.dynamic_slice_in_dim(counts, lax.axis_index("expert"), 1, 0)
    return factor(grams, count, place[None].astype(jnp.int32))[None]


def solution(mesh):
    placed = (P(("dp", "expert"), None, None), P(("dp", "expert"), None))
    return jax.shard_map(
        shards, mesh=mesh, in_specs=placed, out_specs=P("expert", "dp", None), check_vma=False
    )
```

time: 1050 us -> 496 us (0.47)
  other arithmetic: 416 us -> 21 us
  Pallas kernels: 0 us -> 105 us
  waiting for transfers between devices: 303 us -> 199 us
  blocking collectives: 129 us -> 76.7 us
  local copies, waits for them, and re-layouts: 95.2 us -> 47.5 us
  matrix products: 71.9 us -> 24.7 us
  between operations: 22.9 us -> 0.45 us
  starting transfers between devices: 4.6 us -> 20.4 us
    another operation x62 -> x3, other arithmetic: 390 us -> 10.1 us  [the longest x43 257 us: shards(): corner = jnp.linalg.cholesky(panel_rows[:, :block_rows])]
    psum x4 -> x0, waiting for transfers between devices: 243 us -> none  [broadcast(): return lax.psum(jnp.where(mine, value, jnp.zeros_like(value)), axis)]
    all_to_all x1, waiting for transfers between devices: 8.45 us -> 137 us  [shards(): lax.all_to_all(outgoing.reshape(owners, capacity, features), 'expert', sp...]
    all_to_all x1 -> x0, blocking collectives: 120 us -> none  [shards(): lax.all_to_all(outgoing.reshape(owners, capacity, features), 'expert', sp...]
    pallas_call x0 -> x1, Pallas kernels: none -> 105 us  [factor(): pl.pallas_call(functools.partial(factor_kernel, size, parts), out_shape=j...]
    psum x1, blocking collectives: 8.93 us -> 76.7 us  [shards(): counts = lax.psum(jnp.sum(chosen, axis=0).astype(f32), ('dp', 'expert'))]
    ppermute x0 -> x12, waiting for transfers between devices: none -> 61.6 us  [the longest x4 61.6 us: shards(): mine = mine + lax.ppermute(mine, 'dp', [(i, i ^ 2) for i in range(parts)])]
    reduce_scatter x1 -> x0, waiting for transfers between devices: 51.5 us -> none  [shards(): lax.psum_scatter(lax.dot_general(received, received, contract, preferred_...]
  transfers between devices with their start and end apart: 6 -> 13, of which waited for: 6 -> 2; matrix products, arithmetic and copies ran while one was open for 2% -> 4% of each run, Pallas kernels for 0% -> 0%
where the time goes in v1:
time: 496 us; the launch traced here: 494 us
  waiting for transfers between devices  199 us (40%)
  Pallas kernels  105 us (21%)
  blocking collectives  76.7 us (15%)
  local copies, waits for them, and re-layouts  47.5 us (10%)
  matrix products  24.7 us (5%)
  other arithmetic  21 us (4%)
  starting transfers between devices  20.4 us (4%)
    all_to_all x1, waiting for transfers between devices, shards(): lax.all_to_all(outgoing.reshape(owners, capacity, features), 'expert', sp...  137 us
    pallas_call x1, Pallas kernels, factor(): pl.pallas_call(functools.partial(factor_kernel, size, parts), out_shape=j...  105 us
    psum x1, blocking collectives, shards(): counts = lax.psum(jnp.sum(chosen, axis=0).astype(f32), ('dp', 'expert'))  76.7 us
    ppermute x4, waiting for transfers between devices, shards(): mine = mine + lax.ppermute(mine, 'dp', [(i, i ^ 2) for i in range(parts)])  61.6 us
    scatter x1, local copies, waits for them, and re-layouts, shards(): outgoing.at[target].set(hidden.reshape(-1, features), mode='drop')  44 us
    dot_general x4, matrix products, shards(): lax.dot_general(received[:, c * share:], received[:, c * share:(c + 1) *...  24.7 us
    all_to_all x1, starting transfers between devices, shards(): lax.all_to_all(outgoing.reshape(owners, capacity, features), 'expert', sp...  11.7 us
    another operation x3, other arithmetic  10.1 us
  transfers between devices with their start and end apart: 13, of which 2 were waited for; matrix products, arithmetic and copies ran while one was open for 4% of the time, Pallas kernels for 0%

profile of v1, /device:TPU:1, one launch (start us, length us, event | category | flops | bytes accessed | tf_op | source)
XLA Modules:
  0.0 494.4 jit_solution(2805831213196866748)
XLA Ops:
  0.0 0.9 copy.3
  1.6 0.3 reshape.186
  2.0 9.5 %reduce-window.6 = s32[32,64,128]{2,1,0:T(8,128)S(1)} reduce-window(s32[32,64,128]{2,1,0:T(8,128)S(1)} %fusion.17, s32[]{:T(128)} %constant.59.clone.1), window={size=1x1x128 pad=0_0x0_0x127_0}, to_apply=%region_2.3 | reduce-window | flops 33292288 | bytes 2097156 | tf_op jit(solution)/shard_map/reduce-window
  11.5 0.9 slice_reduce_fusion
  12.7 0.3 broadcast_add_fusion
  13.0 0.9 fusion.14
  14.2 44.0 %scatter_custom_fusion = bf16[3072,1536]{1,0:T(8,128)(2,1)} fusion(s32[8192]{0:T(1024)S(1)} %bitcast.28, bf16[1024,8,1536]{2,1,0:T(8,128)(2,1)} %param.2, bf16[]{:T(256)} %constant.68.clone.1), kind=kCustom, calls=%fused_computation.1 | custom fusion | bytes 34603008 | tf_op jit(solution)/shard_map/scatter | solution.py:178
  58.2 11.7 %all-to-all-start = ((bf16[32,96,1536]{2,1,0:T(8,128)(2,1)}), bf16[32,96,1536]{2,1,0:T(8,128)(2,1)}, u32[]{:S(2)}, u32[]{:S(2)}) async-start(bf16[32,96,1536]{2,1,0:T(8,128)(2,1)} %bitcast.24), calls=%async_computation | async-start | bytes 18874368 | tf_op jit(solution)/shard_map/all_to_all | solution.py:179
  70.0 136.9 %all-to-all-done = bf16[32,96,1536]{2,1,0:T(8,128)(2,1)} async-done(((bf16[32,96,1536]{2,1,0:T(8,128)(2,1)}), bf16[32,96,1536]{2,1,0:T(8,128)(2,1)}, u32[]{:S(2)}, u32[]{:S(2)}) %all-to-all-start) | async-done | bytes 9437216 | tf_op jit(solution)/shard_map/all_to_all | solution.py:179
  206.9 8.5 %fusion.11 = f32[1536,384]{1,0:T(8,128)S(1)} fusion(bf16[3072,1536]{1,0:T(8,128)(2,1)} %bitcast.6), kind=kOutput, calls=%fused_computation.12 | convolution fusion | flops 3623878656 | bytes 14155776 | tf_op jit(solution)/shard_map/dot_general | solution.py:189
  215.4 6.9 %fusion.2 = f32[1152,384]{1,0:T(8,128)S(1)} fusion(bf16[3072,1536]{1,0:T(8,128)(2,1)} %bitcast.6), kind=kOutput, calls=%fused_computation.3 | convolution fusion | flops 2717908992 | bytes 11206656 | tf_op jit(solution)/shard_map/dot_general | solution.py:189
  222.4 1.6 collective-permute-start
  224.2 5.5 %fusion.4 = f32[768,384]{1,0:T(8,128)S(1)} fusion(bf16[3072,1536]{1,0:T(8,128)(2,1)} %bitcast.6), kind=kOutput, calls=%fused_computation.5 | convolution fusion | flops 1811939328 | bytes 8257536 | tf_op jit(solution)/shard_map/dot_general | solution.py:189
  229.8 0.6 collective-permute-start.6
  230.3 3.8 fusion.7
  234.6 1.5 collective-permute-start.4
  236.4 1.5 collective-permute-start.10
  237.9 61.6 %collective-permute-done.10 = f32[192,384]{1,0:T(8,128)S(1)} collective-permute-done((f32[192,384]{1,0:T(8,128)S(1)}, f32[192,384]{1,0:T(8,128)S(1)}, u32[]{:S(2)}, u32[]{:S(2)}) %collective-permute-start.10) | collective-permute-done | bytes 294944 | tf_op jit(solution)/shard_map/ppermute | solution.py:199
  299.5 1.4 collective-permute-start.11
  301.2 0.6 collective-permute-start.5
  301.8 76.7 %psum.7 = f32[32]{0:T(128)S(1)} all-reduce(f32[32]{0:T(128)S(1)} %convert_element_type.11), channel_id=1, replica_groups=mesh['dp'=4,'expert'=32] {'dp','expert'}, use_global_device_ids=true, to_apply=%region_1.2 | all-reduce | flops 32 | bytes 256 | tf_op jit(solution)/shard_map/psum | solution.py:174
  378.4 0.7 dynamic_slice.27.count_ref
  379.1 1.4 add.130
  380.5 1.0 collective-permute-start.2
  381.5 1.0 broadcast_select_fusion.7
  382.5 0.9 pad_maximum_fusion.3.refs_3_
  383.5 1.1 pad_maximum_fusion.2.refs_2_
  384.6 1.3 broadcast_select_fusion.3
  385.8 1.3 pad_maximum_fusion.1.refs_1_
  387.1 0.3 broadcast_select_fusion.1
  387.4 1.6 pad_maximum_fusion.refs_0_
  389.0 105.2 %factor.1 = f32[384,1536]{1,0:T(8,128)} custom-call(f32[1]{0:T(128)} %dynamic_slice.27.count_ref, s32[1]{0:T(128)} %bitcast.place_ref, f32[1536,384]{1,0:T(8,128)} %pad_maximum_fusion.refs_0_, f32[1152,384]{1,0:T(8,128)} %pad_maximum_fusion.1.refs_1_, f32[768,384]{1,0:T(8,128)} %pad_maximum_fusion.2.refs_2_, f32[384,384]{1,0:T(8,128)} %pad_maximum_fusion.3.refs_3_), custom_call_target="tpu_custom_call" | custom-call | tf_op jit(solution)/shard_map/factor/pallas_call | solution.py:149
  (39 shorter events, 2.6 us)
Async XLA Ops:
  58.2 148.7 %all-to-all-start = ((bf16[32,96,1536]{2,1,0:T(8,128)(2,1)}), bf16[32,96,1536]{2,1,0:T(8,128)(2,1)}, u32[]{:S(2)}, u32[]{:S(2)}) async-start(bf16[32,96,1536]{2,1,0:T(8,128)(2,1)} %bitcast.24), calls=%async_computation | async-start | bytes 18874368 | tf_op jit(solution)/shard_map/all_to_all | solution.py:179
  222.4 11.9 %collective-permute-start = (f32[768,384]{1,0:T(8,128)S(1)}, f32[768,384]{1,0:T(8,128)S(1)}, u32[]{:S(2)}, u32[]{:S(2)}) collective-permute-start(f32[768,384]{1,0:T(8,128)S(1)} %constant_dynamic-slice_fusion.3), channel_id=1, source_target_pairs={{0,32},{32,0},{64,96},{96,64},{1,33},{33,1},{65,97},{97,65},{2,34}... | collective-permute-start | bytes 3538952 | tf_op jit(solution)/shard_map/ppermute | solution.py:198
  224.1 10.5 %collective-permute-start.3 = (f32[576,384]{1,0:T(8,128)S(1)}, f32[576,384]{1,0:T(8,128)S(1)}, u32[]{:S(2)}, u32[]{:S(2)}) collective-permute-start(f32[576,384]{1,0:T(8,128)S(1)} %constant_dynamic-slice_fusion.2), channel_id=1, source_target_pairs={{0,32},{32,0},{64,96},{96,64},{1,33},{33,1},{65,97},{97,65},{2,34}... | collective-permute-start | bytes 2654216 | tf_op jit(solution)/shard_map/ppermute | solution.py:198
  229.8 6.4 %collective-permute-start.6 = (f32[384,384]{1,0:T(8,128)S(1)}, f32[384,384]{1,0:T(8,128)S(1)}, u32[]{:S(2)}, u32[]{:S(2)}) collective-permute-start(f32[384,384]{1,0:T(8,128)S(1)} %constant_dynamic-slice_fusion.1), channel_id=1, source_target_pairs={{0,32},{32,0},{64,96},{96,64},{1,33},{33,1},{65,97},{97,65},{2,34}... | collective-permute-start | bytes 1769480 | tf_op jit(solution)/shard_map/ppermute | solution.py:198
  234.2 2.2 collective-permute-start.9
  234.4 144.7 %collective-permute-start.1 = (f32[768,384]{1,0:T(8,128)S(1)}, f32[768,384]{1,0:T(8,128)}, u32[]{:S(2)}, u32[]{:S(2)}) collective-permute-start(f32[768,384]{1,0:T(8,128)S(1)} %dynamic-slice_add_fusion), channel_id=1, source_target_pairs={{0,64},{32,96},{64,0},{96,32},{1,65},{33,97},{65,1},{97,33},{2,66}... | collective-permute-start | bytes 3538952 | tf_op jit(solution)/shard_map/ppermute | solution.py:199
  234.6 66.5 %collective-permute-start.4 = (f32[576,384]{1,0:T(8,128)S(1)}, f32[576,384]{1,0:T(8,128)S(1)}, u32[]{:S(2)}, u32[]{:S(2)}) collective-permute-start(f32[576,384]{1,0:T(8,128)S(1)} %dynamic-slice_add_fusion.1), channel_id=1, source_target_pairs={{0,64},{32,96},{64,0},{96,32},{1,65},{33,97},{65,1},{97,33},{2,66}... | collective-permute-start | bytes 2654216 | tf_op jit(solution)/shard_map/ppermute | solution.py:199
  236.2 64.7 %collective-permute-start.7 = (f32[384,384]{1,0:T(8,128)S(1)}, f32[384,384]{1,0:T(8,128)S(1)}, u32[]{:S(2)}, u32[]{:S(2)}) collective-permute-start(f32[384,384]{1,0:T(8,128)S(1)} %dynamic-slice_add_fusion.2), channel_id=1, source_target_pairs={{0,64},{32,96},{64,0},{96,32},{1,65},{33,97},{65,1},{97,33},{2,66}... | collective-permute-start | bytes 1769480 | tf_op jit(solution)/shard_map/ppermute | solution.py:199
  236.4 63.1 %collective-permute-start.10 = (f32[192,384]{1,0:T(8,128)S(1)}, f32[192,384]{1,0:T(8,128)S(1)}, u32[]{:S(2)}, u32[]{:S(2)}) collective-permute-start(f32[192,384]{1,0:T(8,128)S(1)} %dynamic-slice_add_fusion.3), channel_id=1, source_target_pairs={{0,64},{32,96},{64,0},{96,32},{1,65},{33,97},{65,1},{97,33},{2,66}... | collective-permute-start | bytes 884744 | tf_op jit(solution)/shard_map/ppermute | solution.py:199
  299.5 82.0 %collective-permute-start.11 = (f32[192,384]{1,0:T(8,128)S(1)}, f32[192,384]{1,0:T(8,128)}, u32[]{:S(2)}, u32[]{:S(2)}) collective-permute-start(f32[192,384]{1,0:T(8,128)S(1)} %add.142), channel_id=1, source_target_pairs={{0,32},{32,0},{64,96},{96,64},{1,33},{33,1},{65,97},{97,65},{2,34}... | collective-permute-start | bytes 884744 | tf_op jit(solution)/shard_map/ppermute | solution.py:200
  301.0 82.4 %collective-permute-start.8 = (f32[384,384]{1,0:T(8,128)S(1)}, f32[384,384]{1,0:T(8,128)S(1)}, u32[]{:S(2)}, u32[]{:S(2)}) collective-permute-start(f32[384,384]{1,0:T(8,128)S(1)} %add.138), channel_id=1, source_target_pairs={{0,32},{32,0},{64,96},{96,64},{1,33},{33,1},{65,97},{97,65},{2,34}... | collective-permute-start | bytes 1769480 | tf_op jit(solution)/shard_map/ppermute | solution.py:200
  301.2 83.4 %collective-permute-start.5 = (f32[576,384]{1,0:T(8,128)S(1)}, f32[576,384]{1,0:T(8,128)}, u32[]{:S(2)}, u32[]{:S(2)}) collective-permute-start(f32[576,384]{1,0:T(8,128)S(1)} %add.134), channel_id=1, source_target_pairs={{0,32},{32,0},{64,96},{96,64},{1,33},{33,1},{65,97},{97,65},{2,34}... | collective-permute-start | bytes 2654216 | tf_op jit(solution)/shard_map/ppermute | solution.py:200
  380.5 6.7 %collective-permute-start.2 = (f32[768,384]{1,0:T(8,128)S(1)}, f32[768,384]{1,0:T(8,128)S(1)}, u32[]{:S(2)}, u32[]{:S(2)}) collective-permute-start(f32[768,384]{1,0:T(8,128)S(1)} %add.130), channel_id=1, source_target_pairs={{0,32},{32,0},{64,96},{96,64},{1,33},{33,1},{65,97},{97,65},{2,34}... | collective-permute-start | bytes 3538952 | tf_op jit(solution)/shard_map/ppermute | solution.py:200
